TPU v7x, 32 devices: a whole 2x2x4 slice. The times are simulated.
32 devices in a mesh: groups: 2 (over y), row: 4 (over x, core), col: 4 (over z).
Axes of the slice: x: 2, y: 2, z: 4, core: 2. Of those that a mesh axis runs over, the one named last changes fastest.
Arguments:
- tile_values: bfloat16 [1536, 128, 128], P(('groups', 'row', 'col')), parts along dimension 0, may hold values from 0 to 1, as said below
- tile_row: int32 [1536], P(('groups', 'row', 'col')), parts along dimension 0, may hold values from 0 to 63, as said below
- tile_column: int32 [1536], P(('groups', 'row', 'col')), parts along dimension 0, may hold values from 0 to 63, as said below
- pair_counts: int32 [8, 4], P(('groups', 'row')), parts along dimension 0, may hold values from 0 to 3, as said below
- start_block: float32 [64, 16384], P(None, ('groups', 'row', 'col')), parts along dimension 1, may hold values from -18 to 18
Outputs:
- vectors: float32 [64, 16384], P(None, ('groups', 'row', 'col')), parts along dimension 1
- vector_images: float32 [64, 16384], P(None, ('groups', 'row', 'col')), parts along dimension 1
There are 2 independent parts, one for each index of `groups`. A program takes and returns all parts, laid end to end along the dimension named above; each array names one. Nothing has to cross between parts.
Inputs may be any that keep to these rules, and one draw needn't show every extreme that they name: `tile_row`: slot t = ((r * 4 + c) * 4 + b) * 4 * 3 + e * 3 + q holds a tile whose row lies in row block r and class e, row index r * 16 + e * 4 + u, and whose column lies in block b and class c, column index b * 16 + c * 4 + v, with u and v below 4. `tile_column`: see tile_row; the tile in slot (r, c, b, e, q) has the swapped row and column of the tile in slot (b, e, r, c, q); where r = b and c = e the slot holds a diagonal tile. `pair_counts`: Symmetric; every draw has row blocks whose pairs all hold 3. `tile_values`: the tile in slot (r, c, b, e, q) is the transpose of the one in slot (b, e, r, c, q); diagonal tiles are symmetric.
All inputs are finite; a program needn't handle non-finite values.
Results may differ from a plain program's by a relative error of at most 0.0004.
The roundings to bfloat16 on the way count: a program that leaves them out, or rounds other values in their place, can miss the bound.
Values may be sent and summed in bfloat16 or wider, within the bound.
A program may use at most 64 MiB of HBM per device.

v0:
```python
import jax
import jax.numpy as jnp
from jax import lax
from jax.sharding import PartitionSpec as P

Q = 3
ITERS = 2
FILT = 4


highest = lax.Precision.HIGHEST


def inner_mean(left_rows, right_rows, rows_total):
    return jnp.einsum("mn,pn->mp", left_rows, right_rows, precision=highest) / rows_total


def small_problem(gram_basis, gram_image, width_k):
    lower_factor = jnp.linalg.cholesky(gram_basis)
    symmetric = 0.5 * (gram_image + gram_image.T)
    halfway = jax.scipy.linalg.solve_triangular(lower_factor, symmetric, lower=True)
    reduced = jax.scipy.linalg.solve_triangular(lower_factor, halfway.T, lower=True)
    coords = lower_factor[:width_k, :]
    shifted = 2.5 * jnp.eye(gram_basis.shape[0], dtype=jnp.float32) - reduced
    for filtering in range(FILT):
        coords = jnp.dot(coords, shifted, precision=highest)
        factor = jnp.linalg.cholesky(jnp.dot(coords, coords.T, precision=highest))
        coords = jax.scipy.linalg.solve_triangular(factor, coords, lower=True)
    return jax.scipy.linalg.solve_triangular(lower_factor, coords.T, lower=True, trans=1).T


def on_device(tile_values, tile_row, tile_column, pair_counts, start_block):
    column_devices = lax.axis_size("col")
    width_k, own_rows = start_block.shape
    tile_edge = tile_values.shape[1]
    class_tiles = own_rows // tile_edge
    block_tiles = class_tiles * column_devices
    group_slots = column_devices * Q
    rows_total = own_rows * lax.axis_size("row") * column_devices
    slot_index = jnp.arange(tile_values.shape[0], dtype=jnp.int32)
    live_mask = (slot_index % Q < jnp.take(pair_counts[0], slot_index // group_slots)).astype(
        jnp.float32
    )
    local_row = tile_row % block_tiles
    local_column = tile_column % class_tiles
    class_range = jnp.arange(class_tiles, dtype=jnp.int32)[None, :]
    row_spots = ((local_row % class_tiles)[:, None] == class_range).astype(jnp.float32) * live_mask[
        :, None
    ]
    row_places = (local_row[:, None] == jnp.arange(block_tiles, dtype=jnp.int32)[None, :]).astype(
        jnp.float32
    ) * live_mask[:, None]
    row_totals = jnp.sum(tile_values, axis=2, dtype=jnp.float32)
    degree_terms = jnp.einsum("sa,st->ta", row_totals, row_places, precision=highest).reshape(
        block_tiles * tile_edge
    )
    degree = 1.0 + lax.psum_scatter(degree_terms, "col", scatter_dimension=0, tiled=True)
    degree_scale = 1.0 / jnp.sqrt(degree)

    def apply_operator(current):
        scaled_panel = (current * degree_scale[None, :]).astype(jnp.bfloat16)
        start_total = jnp.zeros((width_k, block_tiles, tile_edge), jnp.float32)
        shard_piece = lax.all_gather(scaled_panel, "row", axis=1, tiled=True)
        pieces_here = shard_piece.shape[1] // own_rows

        def one_block(block_step, running_inner):
            block_panel = lax.dynamic_slice_in_dim(
                shard_piece, block_step * own_rows, own_rows, 1
            ).reshape(width_k, class_tiles, tile_edge)
            values = lax.dynamic_slice_in_dim(tile_values, block_step * group_slots, group_slots, 0)
            columns_here = lax.dynamic_slice_in_dim(
                local_column, block_step * group_slots, group_slots, 0
            )
            spots_here = lax.dynamic_slice_in_dim(
                row_spots, block_step * group_slots, group_slots, 0
            )
            chosen = jnp.take(block_panel, columns_here, axis=1)
            products = jnp.einsum(
                "knc,nac->kna", chosen, values, preferred_element_type=jnp.float32
            )
            products = products.reshape(width_k, column_devices, Q, tile_edge)
            spots_here = spots_here.reshape(column_devices, Q, class_tiles)
            placed = jnp.einsum("keqa,equ->keua", products, spots_here, precision=highest)
            return running_inner + placed.reshape(width_k, block_tiles, tile_edge)

        partial_value = lax.fori_loop(0, pieces_here, one_block, start_total)
        summed = lax.psum_scatter(
            partial_value.reshape(width_k, block_tiles * tile_edge),
            "col",
            scatter_dimension=1,
            tiled=True,
        )
        return current - degree_scale[None, :] * (summed + degree_scale[None, :] * current)

    gram_start = lax.psum(inner_mean(start_block, start_block, rows_total), ("row", "col"))
    lower_start = jnp.linalg.cholesky(gram_start)
    current = jax.scipy.linalg.solve_triangular(lower_start, start_block, lower=True)
    imaged = apply_operator(current)
    previous = current
    previous_image = imaged
    projected = jnp.zeros((width_k, width_k), jnp.float32)
    for iteration in range(ITERS):
        if iteration == 0:
            rayleigh = lax.psum(inner_mean(current, imaged, rows_total), ("row", "col"))
        else:
            rayleigh = projected
        residual = imaged - jnp.dot(0.5 * (rayleigh + rayleigh.T), current, precision=highest)
        if iteration == 0:
            basis_rows = jnp.concatenate([current, residual], axis=0)
        else:
            basis_rows = jnp.concatenate([current, residual, previous], axis=0)
        residual_image = apply_operator(residual)
        if iteration == 0:
            images = jnp.concatenate([imaged, residual_image], axis=0)
        else:
            images = jnp.concatenate([imaged, residual_image, previous_image], axis=0)
        gram_basis, gram_image = lax.psum(
            (
                inner_mean(basis_rows, basis_rows, rows_total),
                inner_mean(basis_rows, images, rows_total),
            ),
            ("row", "col"),
        )
        coefficients = small_problem(gram_basis, gram_image, width_k)
        tail_coef = coefficients[:, width_k:]
        projected = jnp.dot(
            jnp.dot(coefficients, gram_image, precision=highest), coefficients.T, precision=highest
        )
        current = jnp.dot(coefficients, basis_rows, precision=highest)
        imaged = jnp.dot(coefficients, images, precision=highest)
        previous = jnp.dot(tail_coef, basis_rows[width_k:], precision=highest)
        previous_image = jnp.dot(tail_coef, images[width_k:], precision=highest)
    return (current, imaged)


def solution(mesh):
    placed = (
        P(("groups", "row", "col"), None, None),
        P(("groups", "row", "col")),
        P(("groups", "row", "col")),
        P(("groups", "row"), None),
        P(None, ("groups", "row", "col")),
    )
    return jax.shard_map(
        on_device,
        mesh=mesh,
        in_specs=placed,
        out_specs=(P(None, ("groups", "row", "col")), P(None, ("groups", "row", "col"))),
        check_vma=False,
    )
```

profile of v0, /device:TPU:0, one launch (start us, length us, event | category | flops | bytes accessed | tf_op | source)
XLA Modules:
  0.0 672.8 jit_solution(8752452667876801497)
XLA Ops:
  14.2 13.7 %all-reduce.5 = f32[2048]{0:T(1024)S(1)} all-reduce(f32[2048]{0:T(1024)S(1)} %convolution_bitcast_fusion.5), channel_id=2, replica_groups=mesh['groups'=2,'row'=4,'col'=4] {'col'}, use_global_device_ids=true, to_apply=%region_4.6.clone | all-reduce | flops 2048 | bytes 16384
  28.1 58.0 %psum.42 = f32[64,64]{0,1:T(8,128)S(1)} all-reduce(f32[64,64]{0,1:T(8,128)S(1)} %convolution_multiply_fusion.5), channel_id=1, replica_groups=mesh['groups'=2,'row'=4,'col'=4] {'row','col'}, use_global_device_ids=true, to_apply=%region_0.1 | all-reduce | flops 4096 | bytes 32768 | tf_op jit(solution)/shard_map/psum | solution.py:95
  86.2 5.8 cholesky.310
  105.8 10.8 %while.47 = (s32[]{:T(128)}, f32[64,16,128]{2,0,1:T(8,128)S(1)}, f32[48,4]{0,1:T(4,128)S(1)}, bf16[48,128,128]{2,1,0:T(8,128)(2,1)S(1)}, bf16[64,2048]{1,0:T(8,1...) while((s32[]{:T(128)}, f32[64,16,128]{2,0,1:T(8,128)S(1)}, ...), condition=%wide.region_6.9_spmd.clone, body=%wide.region_5.8_spmd.clone.sunk | while | flops 30245968 | bytes 5052279 | solution.py:86
  117.5 20.0 %reduce-scatter.4.cloned.1.call-done = f32[64,512]{1,0:T(8,128)} async-done(((f32[64,2048]{1,0:T(8,128)}), f32[64,512]{1,0:T(8,128)}) %reduce-scatter.4.cloned.1.call-update) | async-done | bytes 131088 | tf_op jit(solution)/shard_map/reduce_scatter | solution.py:87
  138.7 58.0 %psum.43 = f32[64,64]{0,1:T(8,128)S(1)} all-reduce(f32[64,64]{0,1:T(8,128)S(1)} %convolution_multiply_fusion.4), channel_id=1, replica_groups=mesh['groups'=2,'row'=4,'col'=4] {'row','col'}, use_global_device_ids=true, to_apply=%region_8.11 | all-reduce | flops 4096 | bytes 32768 | tf_op jit(solution)/shard_map/psum | solution.py:104
  197.1 6.3 all_gather.10
  203.4 14.1 %while.48 = (s32[]{:T(128)}, f32[64,16,128]{2,0,1:T(8,128)S(1)}, f32[48,4]{0,1:T(4,128)S(1)}, bf16[48,128,128]{2,1,0:T(8,128)(2,1)S(1)}, bf16[64,2048]{1,0:T(8,1...) while((s32[]{:T(128)}, f32[64,16,128]{2,0,1:T(8,128)S(1)}, ...), condition=%wide.region_13.16_spmd.clone, body=%wide.region_12.15_spmd.clone.sunk | while | flops 30245968 | bytes 5052279 | solution.py:86
  219.4 18.8 %reduce-scatter.6.cloned.1.call-done = f32[64,512]{1,0:T(8,128)} async-done(((f32[64,2048]{1,0:T(8,128)}), f32[64,512]{1,0:T(8,128)}) %reduce-scatter.6.cloned.1.call-update) | async-done | bytes 131088 | tf_op jit(solution)/shard_map/reduce_scatter | solution.py:87
  240.4 87.3 %all-reduce.13.cloned.1.call-done = (f32[128,128]{0,1:T(8,128)}, f32[128,128]{0,1:T(8,128)}) async-done(((f32[128,128]{0,1:T(8,128)}, f32[128,128]{0,1:T(8,128)}), (f32[128,128]{0,1:T(8,128)}, f32[128,128]{0,1:T(8,128)})) %all-reduce.13.cloned.1.call-update) | async-done | bytes 131088 | tf_op jit(solution)/shard_map/psum | solution.py:117
  329.6 11.7 %cholesky.98 = f32[128,128]{1,0:T(8,128)S(1)} custom-call(f32[128,128]{1,0:T(8,128)S(1)} %broadcast_multiply_fusion.1), custom_call_target="Cholesky" | custom-call | tf_op jit(solution)/shard_map/jit(cholesky)/cholesky | solution.py:19
  342.7 9.8 %custom-call.41 = f32[1,128,128]{1,2,0:T(8,128)S(1)} custom-call(f32[1,128,128]{2,1,0:T(8,128)S(1)} %get-tuple-element.495), custom_call_target="InvertDiagBlocksLowerTriangular" | custom-call | tf_op jit(solution)/shard_map/jit(_solve_triangular)/triangular_solve | solution.py:29
  355.3 5.8 cholesky.321
  381.0 5.8 cholesky.343
  386.9 12.5 %compare_reduce_fusion.5 = pred[]{:T(512)} fusion(f32[64]{0:T(128)S(1)} %select_reduce_fusion.7), kind=kLoop, calls=%fused_computation.244 | loop fusion | flops 127 | bytes 257 | tf_op jit(solution)/shard_map/jit(cholesky)/cholesky | solution.py:27
  419.7 6.4 all_gather.11
  426.1 14.1 %while.49 = (s32[]{:T(128)}, f32[64,16,128]{2,0,1:T(8,128)S(1)}, f32[48,4]{0,1:T(4,128)S(1)}, bf16[48,128,128]{2,1,0:T(8,128)(2,1)S(1)}, bf16[64,2048]{1,0:T(8,1...) while((s32[]{:T(128)}, f32[64,16,128]{2,0,1:T(8,128)S(1)}, ...), condition=%wide.region_22.27_spmd.clone, body=%wide.region_21.26_spmd.clone.sunk | while | flops 30245968 | bytes 5052279 | solution.py:86
  443.0 21.5 %reduce-scatter.8.cloned.1.call-done = f32[64,512]{1,0:T(8,128)} async-done(((f32[64,2048]{1,0:T(8,128)}), f32[64,512]{1,0:T(8,128)}) %reduce-scatter.8.cloned.1.call-update) | async-done | bytes 131088 | tf_op jit(solution)/shard_map/reduce_scatter | solution.py:87
  466.7 90.0 %all-reduce.11.cloned.1.call-done = (f32[192,192]{0,1:T(8,128)}, f32[192,192]{0,1:T(8,128)}) async-done(((f32[192,192]{0,1:T(8,128)}, f32[192,192]{0,1:T(8,128)}), (f32[192,192]{0,1:T(8,128)}, f32[192,192]{0,1:T(8,128)})) %all-reduce.11.cloned.1.call-update) | async-done | bytes 294928 | tf_op jit(solution)/shard_map/psum | solution.py:117
  558.8 11.7 %cholesky.161 = f32[128,128]{1,0:T(8,128)S(1)} custom-call(f32[128,128]{1,0:T(8,128)S(1)} %cholesky.407), custom_call_target="Cholesky" | custom-call | tf_op jit(solution)/shard_map/jit(cholesky)/cholesky | solution.py:19
  570.6 9.8 %custom-call.42 = f32[1,128,128]{1,2,0:T(8,128)S(1)} custom-call(f32[1,128,128]{2,1,0:T(8,128)S(1)} %get-tuple-element.500), custom_call_target="InvertDiagBlocksLowerTriangular" | custom-call | tf_op jit(solution)/shard_map/jit(cholesky)/cholesky | solution.py:19
  589.4 19.9 %custom-call.43 = f32[2,128,128]{1,2,0:T(8,128)S(1)} custom-call(f32[2,128,128]{2,1,0:T(8,128)S(1)} %pad_maximum_fusion.14), custom_call_target="InvertDiagBlocksLowerTriangular" | custom-call | tf_op jit(solution)/shard_map/jit(_solve_triangular)/triangular_solve | solution.py:29
  612.2 5.8 cholesky.365
  638.0 5.8 cholesky.387
  (312 shorter events, 170.3 us)
Async XLA Ops:
  7.2 20.7 %copy-start = (f32[64,512]{1,0:T(8,128)S(1)}, f32[64,512]{1,0:T(8,128)}, u32[]{:S(2)}) copy-start(f32[64,512]{1,0:T(8,128)} %param.26) | copy-start | bytes 393220
  7.2 91.1 %copy-start.9 = (u32[32]{0:T(128)S(1)}, u32[32]{0:T(128)}, u32[]{:S(2)}) copy-start(u32[32]{0:T(128)} %constant.479) | copy-start | bytes 388
  7.2 98.6 %copy-start.1 = (bf16[48,128,128]{2,1,0:T(8,128)(2,1)S(1)}, bf16[48,128,128]{2,1,0:T(8,128)(2,1)}, u32[]{:S(2)}) copy-start(bf16[48,128,128]{2,1,0:T(8,128)(2,1)} %param.22) | copy-start | bytes 4718596
  7.2 98.6 %copy-start.8 = (s32[48]{0:T(128)S(1)}, s32[48]{0:T(128)}, u32[]{:S(2)}) copy-start(s32[48]{0:T(128)} %param.24) | copy-start | bytes 580
  7.2 130.2 %reduce-scatter.4.cloned.1.call-start = ((), (), s32[]{:S(2)}) async-start(), calls=%async_computation.3 | async-start | bytes 655360 | tf_op jit(solution)/shard_map/reduce_scatter | solution.py:87
  117.4 120.7 %reduce-scatter.6.cloned.1.call-start = ((), (), s32[]{:S(2)}) async-start(), calls=%async_computation.4 | async-start | bytes 655360 | tf_op jit(solution)/shard_map/reduce_scatter | solution.py:87
  218.3 109.4 %all-reduce.13.cloned.1.call-start = ((), (), s32[]{:S(2)}) async-start(), calls=%async_computation.7 | async-start | bytes 262144 | tf_op jit(solution)/shard_map/psum | solution.py:117
  240.1 224.4 %reduce-scatter.8.cloned.1.call-start = ((), (), s32[]{:S(2)}) async-start(), calls=%async_computation.5 | async-start | bytes 655360 | tf_op jit(solution)/shard_map/reduce_scatter | solution.py:87
  342.7 75.6 %copy-start.7 = (f32[128,128]{0,1:T(8,128)S(1)}, f32[128,128]{0,1:T(8,128)}, u32[]{:S(2)}) copy-start(f32[128,128]{0,1:T(8,128)} %get-tuple-element.485) | copy-start | bytes 196612
  418.8 7.3 %copy-start.2 = (f32[64,512]{1,0:T(8,128)}, f32[64,512]{1,0:T(8,128)S(1)}, u32[]{:S(2)}) copy-start(f32[64,512]{1,0:T(8,128)S(1)} %fusion.34) | copy-start | bytes 393220
  419.1 7.1 %copy-start.4 = (f32[64,512]{1,0:T(8,128)}, f32[64,512]{1,0:T(8,128)S(1)}, u32[]{:S(2)}) copy-start(f32[64,512]{1,0:T(8,128)S(1)} %fusion.31) | copy-start | bytes 393220
  440.2 1.2 copy-start.3
  440.2 25.2 %copy-start.5 = (f32[64,512]{1,0:T(8,128)S(1)}, f32[64,512]{1,0:T(8,128)}, u32[]{:S(2)}) copy-start(f32[64,512]{1,0:T(8,128)} %copy-done.4) | copy-start | bytes 393220
  441.1 115.6 %all-reduce.11.cloned.1.call-start = ((), (), s32[]{:S(2)}) async-start(), calls=%async_computation.6 | async-start | bytes 786432 | tf_op jit(solution)/shard_map/psum | solution.py:117
  558.7 50.6 %copy-start.6 = (f32[192,192]{0,1:T(8,128)S(1)}, f32[192,192]{0,1:T(8,128)}, u32[]{:S(2)}) copy-start(f32[192,192]{0,1:T(8,128)} %get-tuple-element.484) | copy-start | bytes 442372
Sparse Core Ops, SparseCore 0:
  117.5 19.8 reduce-scatter.3
  218.5 19.6 reduce-scatter.5
  242.3 85.4 all-reduce.12
  441.2 23.2 reduce-scatter.7
  467.8 88.8 all-reduce.10
where the time goes:
time: 681 us; the launch traced here: 673 us
  waiting for transfers between devices  238 us (35%)
  other arithmetic  205 us (30%)
  blocking collectives  148 us (22%)
  matrix products  38.4 us (6%)
  local copies, waits for them, and re-layouts  25.2 us (4%)
  between operations  17.1 us (3%)
    psum x2, waiting for transfers between devices, on_device(): lax.psum((inner_mean(basis_rows, basis_rows, rows_total), inner_mean(basi...  177 us
    another operation x24, other arithmetic, small_problem(): factor = jnp.linalg.cholesky(jnp.dot(coords, coords.T, precision=highest))  64 us
    reduce_scatter x3, waiting for transfers between devices, apply_operator(): lax.psum_scatter(partial_value.reshape(width_k, block_tiles * tile_edge),...  60.3 us
    psum x1, blocking collectives, on_device(): rayleigh = lax.psum(inner_mean(current, imaged, rows_total), ('row', 'col'))  58 us
    psum x1, blocking collectives, on_device(): lax.psum(inner_mean(start_block, start_block, rows_total), ('row', 'col'))  58 us
    another operation x16, other arithmetic, small_problem(): coords = jax.scipy.linalg.solve_triangular(factor, coords, lower=True)  44.4 us
    another operation x10, other arithmetic, small_problem(): lower_factor = jnp.linalg.cholesky(gram_basis)  41.1 us
    another operation x8, other arithmetic, small_problem(): jax.scipy.linalg.solve_triangular(lower_factor, coords.T, lower=True, tra...  30.5 us
  transfers between devices with their start and end apart: 5, of which 5 were waited for; matrix products, arithmetic and copies ran while one was open for 0% of the time, Pallas kernels for 0%

commit v1 on v0

v1 whole, which is shorter than its diff:
```python
import functools

import jax
import jax.numpy as jnp
from jax import lax
from jax.experimental import pallas as pl
from jax.experimental.pallas import tpu as pltpu
from jax.sharding import PartitionSpec as P

Q = 3
TILE = 128
MESH = pl.DeviceIdType.MESH
highest = lax.Precision.HIGHEST
f32 = jnp.float32


def mm(left, right):
    return jnp.dot(left, right, precision=highest, preferred_element_type=f32)


def mt(left, right):
    return lax.dot_general(
        left, right, (((1,), (1,)), ((), ())), precision=highest, preferred_element_type=f32
    )


def eye(rows, columns=None):
    columns = rows if columns is None else columns
    shape = (rows, columns)
    return (
        lax.broadcasted_iota(jnp.int32, shape, 0) == lax.broadcasted_iota(jnp.int32, shape, 1)
    ).astype(f32)


def factor_inverse(matrix):
    width = matrix.shape[0]
    work = jnp.concatenate([matrix, eye(width)], axis=1)
    row_id = lax.broadcasted_iota(jnp.int32, (width, 1), 0)
    for j in range(width - 1):
        pivot = work[j : j + 1, :]
        column = work[:, j : j + 1]
        scaled = jnp.where(row_id > j, column * (1.0 / pivot[:, j : j + 1]), 0.0)
        work = work - scaled * pivot
    diagonal = jnp.sum(work[:, :width] * eye(width), axis=1, keepdims=True)
    return work[:, width:] * lax.rsqrt(diagonal)


def filtered(reduced, width_k):
    size = reduced.shape[0]
    shifted = 2.5 * eye(size) - reduced
    coords = mm(shifted[:width_k], shifted)
    coords = mm(factor_inverse(mt(coords, coords)), coords)
    coords = mm(mm(coords, shifted), shifted)
    return mm(factor_inverse(mt(coords, coords)), coords)


def sym(matrix):
    return 0.5 * (matrix + matrix.T)


def kernel(
    sizes,
    tiles,
    spots,
    start,
    current_out,
    imaged_out,
    panels,
    sums,
    arrived,
    degree_sums,
    degree_arrived,
    *rest,
):
    rows, columns, width_k, class_tiles, rows_total = sizes
    devices = rows * columns
    ar_bufs, sems = rest[:12], rest[12:]
    my_row, my_col = lax.axis_index("row"), lax.axis_index("col")
    me = my_row * columns + my_col
    own = class_tiles * TILE
    flat = devices <= 16

    def peer_flat(step):
        other = lax.rem(me + step, devices)
        return {"row": other // columns, "col": lax.rem(other, columns)}

    barrier = pltpu.get_barrier_semaphore()
    if flat:
        for step in range(1, devices):
            pl.semaphore_signal(barrier, inc=1, device_id=peer_flat(step), device_id_type=MESH)
        pl.semaphore_wait(barrier, devices - 1)
    else:
        for step in range(1, rows):
            pl.semaphore_signal(
                barrier, inc=1, device_id={"row": lax.rem(my_row + step, rows)}, device_id_type=MESH
            )
        for step in range(1, columns):
            pl.semaphore_signal(
                barrier,
                inc=1,
                device_id={"col": lax.rem(my_col + step, columns)},
                device_id_type=MESH,
            )
        pl.semaphore_wait(barrier, rows + columns - 2)

    def send(source, target, send_sem, recv_sem, device):
        copy = pltpu.make_async_remote_copy(
            src_ref=source,
            dst_ref=target,
            send_sem=send_sem,
            recv_sem=recv_sem,
            device_id=device,
            device_id_type=MESH,
        )
        copy.start()
        return copy

    def total_start(stage, value):
        source, landed, result = ar_bufs[3 * stage : 3 * stage + 3]
        sem = sems[stage]
        if not flat:
            source[...] = value
            return [
                send(
                    source,
                    landed.at[my_col],
                    sem.at[0, step],
                    sem.at[1, step],
                    {"col": lax.rem(my_col + step, columns)},
                )
                for step in range(1, columns)
            ]
        piece = width_k // devices
        for i in range(devices):
            source[i] = value[i * piece : (i + 1) * piece]
        return [
            send(
                source.at[lax.rem(me + step, devices)],
                landed.at[step],
                sem.at[0, step],
                sem.at[1, step],
                peer_flat(step),
            )
            for step in range(1, devices)
        ]

    def total_finish(stage, copies):
        source, landed, result = ar_bufs[3 * stage : 3 * stage + 3]
        sem = sems[stage]
        if not flat:
            landed[my_col] = source[...]
            for copy in copies:
                copy.wait()
            value = landed[0]
            for i in range(1, columns):
                value = value + landed[i]
            result[my_row] = value
            copies = [
                send(
                    result.at[my_row],
                    result.at[my_row],
                    sem.at[2, step],
                    sem.at[3, step],
                    {"row": lax.rem(my_row + step, rows)},
                )
                for step in range(1, rows)
            ]
            for copy in copies:
                copy.wait()
            value = result[0]
            for i in range(1, rows):
                value = value + result[i]
            return value
        value = source[me]
        for step, copy in enumerate(copies):
            copy.wait_recv()
            value = value + landed[step + 1]
        result[me] = value
        second = [
            send(
                result.at[me], result.at[me], sem.at[2, step], sem.at[3, step], peer_flat(step)
            )
            for step in range(1, devices)
        ]
        for copy in copies:
            copy.wait_send()
        for copy in second:
            copy.wait()
        return jnp.concatenate([result[i] for i in range(devices)], axis=0)

    def total(stage, value):
        return total_finish(stage, total_start(stage, value))

    def sum_start(source, target, sem):
        return [
            send(
                source.at[lax.rem(my_row + step, rows)],
                target.at[step],
                sem.at[0, step],
                sem.at[1, step],
                {"row": lax.rem(my_row + step, rows)},
            )
            for step in range(1, rows)
        ]

    def sum_finish(source, target, copies):
        value = source[my_row]
        for step, copy in enumerate(copies):
            copy.wait()
            value = value + target[step + 1]
        return jnp.concatenate([value[v] for v in range(class_tiles)], axis=1)

    inverse_total = 1.0 / rows_total
    start_copies = total_start(0, mt(start[...], start[...]) * inverse_total)

    degree_sums[...] = jnp.zeros_like(degree_sums)
    ones = jnp.ones((16, TILE), jnp.bfloat16)

    def degree_step(pair, carry):
        block, group = pair // columns, lax.rem(pair, columns)
        for q in range(Q):
            slot = pair * Q + q
            part = jnp.dot(ones, tiles[slot], preferred_element_type=f32)[:8]
            for v in range(class_tiles):
                degree_sums[block, v] += part * spots[slot * (class_tiles + 1) + 1 + v].astype(f32)
        return carry

    lax.fori_loop(0, rows * columns, degree_step, 0)
    degree_copies = sum_start(degree_sums, degree_arrived, sems[4])
    current = mm(factor_inverse(total_finish(0, start_copies)), start[...])
    degree = 1.0 + sum_finish(degree_sums, degree_arrived, degree_copies)[:1]
    scale = 1.0 / jnp.sqrt(degree)

    def operate(stage, value):
        panel_ref, sum_ref, arrived_ref = panels.at[stage], sums.at[stage], arrived.at[stage]
        gather_sem, sum_sem = sems[5 + 2 * stage], sems[6 + 2 * stage]
        panel = (value * scale).astype(jnp.bfloat16)
        for v in range(class_tiles):
            panel_ref[my_col, v] = panel[:, v * TILE : (v + 1) * TILE]
        copies = [
            send(
                panel_ref.at[my_col],
                panel_ref.at[my_col],
                gather_sem.at[0, step],
                gather_sem.at[1, step],
                {"col": lax.rem(my_col + step, columns)},
            )
            for step in range(1, columns)
        ]
        sum_ref[...] = jnp.zeros_like(sum_ref)
        for step in range(columns):
            if step:
                copies[step - 1].wait_recv()
            group = lax.rem(my_col + columns - step, columns)

            def block_step(block, carry):
                for q in range(Q):
                    slot = (block * columns + group) * Q + q
                    base = slot * (class_tiles + 1)
                    chosen = panel_ref[group, 0]
                    for u in range(1, class_tiles):
                        chosen = jnp.where(spots[base] == u, panel_ref[group, u], chosen)
                    part = jnp.dot(chosen, tiles[slot], preferred_element_type=f32)
                    for v in range(class_tiles):
                        sum_ref[block, v] += part * spots[base + 1 + v].astype(f32)
                return carry

            lax.fori_loop(0, rows, block_step, 0)
        for copy in copies:
            copy.wait_send()
        summed = sum_finish(sum_ref, arrived_ref, sum_start(sum_ref, arrived_ref, sum_sem))
        return value - scale * (summed + scale * value)

    k = width_k
    imaged = operate(0, current)
    rayleigh = sym(total(1, mt(current, imaged) * inverse_total))
    residual = imaged - mm(rayleigh, current)
    residual_image = operate(1, residual)
    local = jnp.concatenate(
        [
            mt(residual, jnp.concatenate([current, residual], axis=0)),
            mt(residual, jnp.concatenate([imaged, residual_image], axis=0)),
            mt(current, jnp.concatenate([residual_image, residual_image], axis=0)),
        ],
        axis=1,
    )
    sent = total(2, local * inverse_total)
    g21, g22 = sent[:, :k], sent[:, k : 2 * k]
    h21 = 0.5 * (sent[:, 2 * k : 3 * k] + sent[:, 4 * k : 5 * k].T)
    h22 = sym(sent[:, 3 * k : 4 * k])
    gram = jnp.concatenate(
        [
            jnp.concatenate([eye(k), g21.T], axis=1),
            jnp.concatenate([g21, g22], axis=1),
        ],
        axis=0,
    )
    hmat = jnp.concatenate(
        [
            jnp.concatenate([rayleigh, h21.T], axis=1),
            jnp.concatenate([h21, h22], axis=1),
        ],
        axis=0,
    )
    w22 = factor_inverse(g22 - mt(g21, g21))
    w21 = -mm(w22, g21)
    inverse = jnp.concatenate(
        [eye(k, 2 * k), jnp.concatenate([w21, w22], axis=1)], axis=0
    )
    coefficients = mm(filtered(mt(mm(inverse, hmat), inverse), k), inverse)
    basis = jnp.concatenate([current, residual], axis=0)
    images = jnp.concatenate([imaged, residual_image], axis=0)
    tail = coefficients[:, k:]
    current, imaged = mm(coefficients, basis), mm(coefficients, images)
    previous, previous_image = mm(tail, residual), mm(tail, residual_image)
    from_left = mm(coefficients, hmat)
    rayleigh = sym(mt(from_left, coefficients))
    h31 = mt(from_left[:, k:], tail).T
    h33 = sym(mt(mm(tail, h22), tail))
    g31 = mt(mm(coefficients, gram)[:, k:], tail).T
    g33 = sym(mt(mm(tail, g22), tail))

    residual = imaged - mm(rayleigh, current)
    residual_image = operate(2, residual)
    local = jnp.concatenate(
        [
            mt(residual, jnp.concatenate([current, residual], axis=0)),
            mt(residual, jnp.concatenate([imaged, residual_image], axis=0)),
            mt(residual, jnp.concatenate([previous, previous_image], axis=0)),
            mt(residual_image, jnp.concatenate([current, previous], axis=0)),
        ],
        axis=1,
    )
    sent = total(3, local * inverse_total)
    g21, g22 = sent[:, :k], sent[:, k : 2 * k]
    h21 = 0.5 * (sent[:, 2 * k : 3 * k] + sent[:, 6 * k : 7 * k])
    h22 = sym(sent[:, 3 * k : 4 * k])
    g32 = sent[:, 4 * k : 5 * k].T
    h32 = 0.5 * (sent[:, 5 * k : 6 * k] + sent[:, 7 * k : 8 * k]).T
    w22 = factor_inverse(g22 - mt(g21, g21))
    l32 = mt(g32 - mt(g31, g21), w22)
    w33 = factor_inverse(g33 - mt(g31, g31) - mt(l32, l32))
    w21 = -mm(w22, g21)
    w31 = -mm(w33, g31 + mm(l32, w21))
    w32 = -mm(w33, mm(l32, w22))
    hmat = jnp.concatenate(
        [
            jnp.concatenate([rayleigh, h21.T, h31.T], axis=1),
            jnp.concatenate([h21, h22, h32.T], axis=1),
            jnp.concatenate([h31, h32, h33], axis=1),
        ],
        axis=0,
    )
    inverse = jnp.concatenate(
        [
            eye(k, 3 * k),
            jnp.concatenate([w21, w22, jnp.zeros((k, k), f32)], axis=1),
            jnp.concatenate([w31, w32, w33], axis=1),
        ],
        axis=0,
    )
    coefficients = mm(filtered(mt(mm(inverse, hmat), inverse), k), inverse)
    current_out[...] = mm(coefficients, jnp.concatenate([current, residual, previous], axis=0))
    imaged_out[...] = mm(
        coefficients, jnp.concatenate([imaged, residual_image, previous_image], axis=0)
    )


def on_device(tile_values, tile_row, tile_column, pair_counts, start_block):
    columns, rows = lax.axis_size("col"), lax.axis_size("row")
    width_k, own = start_block.shape
    class_tiles = own // TILE
    devices = rows * columns
    slots = tile_values.shape[0]
    live = jnp.arange(Q, dtype=jnp.int32)[None, :] < pair_counts[0][:, None]
    live = jnp.broadcast_to(live[:, None, :], (rows, columns, Q)).reshape(slots)
    here = (tile_column % class_tiles)[:, None] == jnp.arange(class_tiles, dtype=jnp.int32)
    spots = jnp.concatenate(
        [(tile_row % class_tiles)[:, None], (here & live[:, None]).astype(jnp.int32)], axis=1
    ).reshape(-1)
    sizes = (rows, columns, width_k, class_tiles, own * devices)
    flat = devices <= 16
    scratch = [
        pltpu.VMEM((3, columns, class_tiles, width_k, TILE), jnp.bfloat16),
        pltpu.VMEM((3, rows, class_tiles, width_k, TILE), f32),
        pltpu.VMEM((3, rows, class_tiles, width_k, TILE), f32),
        pltpu.VMEM((rows, class_tiles, 8, TILE), f32),
        pltpu.VMEM((rows, class_tiles, 8, TILE), f32),
    ]
    for width in (width_k, width_k, 6 * width_k, 8 * width_k):
        if flat:
            scratch += [pltpu.VMEM((devices, width_k // devices, width), f32)] * 3
        else:
            scratch += [
                pltpu.VMEM((width_k, width), f32),
                pltpu.VMEM((columns, width_k, width), f32),
                pltpu.VMEM((rows, width_k, width), f32),
            ]
    most = devices if flat else max(rows, columns)
    scratch += [pltpu.SemaphoreType.DMA((4, most))] * 4
    scratch += [pltpu.SemaphoreType.DMA((2, rows))]
    for stage in range(3):
        scratch += [pltpu.SemaphoreType.DMA((2, columns)), pltpu.SemaphoreType.DMA((2, rows))]
    vmem = pl.BlockSpec(memory_space=pltpu.VMEM)
    return pl.pallas_call(
        functools.partial(kernel, sizes),
        out_shape=(
            jax.ShapeDtypeStruct((width_k, own), f32),
            jax.ShapeDtypeStruct((width_k, own), f32),
        ),
        in_specs=[vmem, pl.BlockSpec(memory_space=pltpu.SMEM), vmem],
        out_specs=(vmem, vmem),
        scratch_shapes=scratch,
        compiler_params=pltpu.CompilerParams(
            collective_id=0, has_side_effects=True, vmem_limit_bytes=52 * 1024 * 1024
        ),
    )(tile_values, spots, start_block)


def solution(mesh):
    split = ("groups", "row", "col")
    placed = (P(split, None, None), P(split), P(split), P(("groups", "row"), None), P(None, split))
    return jax.shard_map(
        on_device,
        mesh=mesh,
        in_specs=placed,
        out_specs=(P(None, split), P(None, split)),
        check_vma=False,
    )
```

time: 681 us -> 147 us (0.22); the launches traced: 673 us -> 147 us
  waiting for transfers between devices: 238 us -> 0 us
  other arithmetic: 205 us -> 2.07 us
  blocking collectives: 148 us -> 0 us
  Pallas kernels: 0 us -> 141 us
  matrix products: 38.4 us -> 0 us
  local copies, waits for them, and re-layouts: 25.2 us -> 3.94 us
  between operations: 17.1 us -> 0.67 us
    another operation x63 -> x0, other arithmetic: 192 us -> none  [the longest x24 64 us: small_problem(): factor = jnp.linalg.cholesky(jnp.dot(coords, coords.T, precision=highest))]
    psum x2 -> x0, waiting for transfers between devices: 177 us -> none  [on_device(): lax.psum((inner_mean(basis_rows, basis_rows, rows_total), inner_mean(basi...]
    pallas_call x0 -> x1, Pallas kernels: none -> 141 us  [on_device(): pl.pallas_call(functools.partial(kernel, sizes), out_shape=(jax.ShapeDtyp...]
    psum x2 -> x0, blocking collectives: 116 us -> none  [the longest x1 58 us: on_device(): rayleigh = lax.psum(inner_mean(current, imaged, rows_total), ('row', 'col'))]
    reduce_scatter x3 -> x0, waiting for transfers between devices: 60.3 us -> none  [apply_operator(): lax.psum_scatter(partial_value.reshape(width_k, block_tiles * tile_edge),...]
    dot_general x57 -> x0, matrix products: 31.4 us -> none  [the longest x12 13.9 us: one_block(): jnp.einsum('keqa,equ->keua', products, spots_here, precision=highest)]
    all_gather x3 -> x0, blocking collectives: 18.5 us -> none  [apply_operator(): shard_piece = lax.all_gather(scaled_panel, 'row', axis=1, tiled=True)]
    unnamed x1 -> x0, blocking collectives: 13.7 us -> none
  transfers between devices with their start and end apart: 5 -> 0, of which waited for: 5 -> 0; matrix products, arithmetic and copies ran while one was open for 0% -> 0% of each run, Pallas kernels for 0% -> 0%
where the time goes in v1:
time: 147 us
  Pallas kernels  141 us (96%)
  local copies, waits for them, and re-layouts  3.94 us (3%)
  other arithmetic  2.07 us (1%)
    pallas_call x1, Pallas kernels, on_device(): pl.pallas_call(functools.partial(kernel, sizes), out_shape=(jax.ShapeDtyp...  141 us
    unnamed x6, local copies, waits for them, and re-layouts  3.62 us

profile of v1, /device:TPU:0, one launch (start us, length us, event | category | flops | bytes accessed | tf_op | source)
XLA Modules:
  0.0 147.2 jit_solution(1241450149803306914)
XLA Ops:
  0.6 0.7 fusion.2
  1.3 0.7 and_select_fusion
  2.0 0.7 iota_compare_fusion
  2.7 0.1 and.21
  2.8 0.1 copy.9
  2.9 0.1 reshape.29.spots
  3.0 0.0 copy-start
  3.0 1.4 copy-done
  4.4 0.0 copy-start.1
  4.5 0.9 copy-done.1
  5.4 140.6 %shard_map.68 = (f32[64,512]{1,0:T(8,128)S(1)}, f32[64,512]{1,0:T(8,128)S(1)}) custom-call(bf16[48,128,128]{2,1,0:T(8,128)(2,1)S(1)} %copy-done, s32[240]{0:T(256)S(1)} %reshape.29.spots, f32[64,512]{1,0:T(8,128)S(1)} %copy-done.1), custom_call_target="tpu_custom_call" | custom-call | tf_op jit(solution)/shard_map/pallas_call | solution.py:405
  145.9 0.7 copy.12
  146.6 0.7 copy.13
  (3 shorter events, 0.0 us)
Async XLA Ops:
  3.0 1.4 copy-start
  4.4 0.9 copy-start.1

commit v2 on v1

--- a/solution.py
+++ b/solution.py
@@ -9,6 +9,8 @@
 
 Q = 3
 TILE = 128
+PIVOTS = 8
+HALVES = 2
 MESH = pl.DeviceIdType.MESH
 highest = lax.Precision.HIGHEST
 f32 = jnp.float32
@@ -34,13 +36,38 @@
 
 def factor_inverse(matrix):
     width = matrix.shape[0]
-    work = jnp.concatenate([matrix, eye(width)], axis=1)
-    row_id = lax.broadcasted_iota(jnp.int32, (width, 1), 0)
-    for j in range(width - 1):
-        pivot = work[j : j + 1, :]
-        column = work[:, j : j + 1]
-        scaled = jnp.where(row_id > j, column * (1.0 / pivot[:, j : j + 1]), 0.0)
-        work = work - scaled * pivot
+    lanes = 2 * width
+    groups = width // 8
+    work = jnp.concatenate([matrix, eye(width)], axis=1).reshape(groups, 8, lanes)
+    shape = (groups, 8, lanes)
+    row_id = 8 * lax.broadcasted_iota(jnp.int32, shape, 0) + lax.broadcasted_iota(
+        jnp.int32, shape, 1
+    )
+    for first in range(0, width, PIVOTS):
+        pivots, columns, entries = [], [], []
+        for i in range(PIVOTS):
+            j = first + i
+            pivots.append(jnp.broadcast_to(work[j // 8, j % 8 : j % 8 + 1], (8, lanes)))
+            columns.append(jnp.broadcast_to(work[:, :, j : j + 1], shape))
+            entries.append(
+                [
+                    jnp.broadcast_to(pivots[i][:, first + m : first + m + 1], (8, lanes))
+                    for m in range(i + 1)
+                ]
+            )
+        for i in range(PIVOTS):
+            recip = 1.0 / entries[i][i]
+            scaled = jnp.where(row_id > first + i, columns[i] * recip[None], 0.0)
+            work = work - scaled * pivots[i][None]
+            ratios = [None] * PIVOTS
+            for m in range(i + 1, PIVOTS):
+                ratios[m] = entries[m][i] * recip
+            for m in range(i + 1, PIVOTS):
+                pivots[m] = pivots[m] - ratios[m] * pivots[i]
+                columns[m] = columns[m] - ratios[m][None] * columns[i]
+                for n in range(i + 1, m + 1):
+                    entries[m][n] = entries[m][n] - ratios[m] * entries[n][i]
+    work = work.reshape(width, lanes)
     diagonal = jnp.sum(work[:, :width] * eye(width), axis=1, keepdims=True)
     return work[:, width:] * lax.rsqrt(diagonal)
 
@@ -61,7 +88,9 @@
 def kernel(
     sizes,
     tiles,
-    spots,
+    tile_rows,
+    tile_columns,
+    counts,
     start,
     current_out,
     imaged_out,
@@ -74,7 +103,7 @@
 ):
     rows, columns, width_k, class_tiles, rows_total = sizes
     devices = rows * columns
-    ar_bufs, sems = rest[:12], rest[12:]
+    ar_bufs, sems = rest[:18], rest[18:]
     my_row, my_col = lax.axis_index("row"), lax.axis_index("col")
     me = my_row * columns + my_col
     own = class_tiles * TILE
@@ -210,6 +239,14 @@
             value = value + target[step + 1]
         return jnp.concatenate([value[v] for v in range(class_tiles)], axis=1)
 
+    def weights(slot, block, q):
+        place = lax.rem(tile_columns[slot], class_tiles)
+        live = counts[0, block] > q
+        return [
+            jnp.where(jnp.logical_and(live, place == v), 1.0, 0.0).astype(f32)
+            for v in range(class_tiles)
+        ]
+
     inverse_total = 1.0 / rows_total
     start_copies = total_start(0, mt(start[...], start[...]) * inverse_total)
 
@@ -221,73 +258,98 @@
         for q in range(Q):
             slot = pair * Q + q
             part = jnp.dot(ones, tiles[slot], preferred_element_type=f32)[:8]
-            for v in range(class_tiles):
-                degree_sums[block, v] += part * spots[slot * (class_tiles + 1) + 1 + v].astype(f32)
+            for v, weight in enumerate(weights(slot, block, q)):
+                degree_sums[block, v] += part * weight
         return carry
 
     lax.fori_loop(0, rows * columns, degree_step, 0)
-    degree_copies = sum_start(degree_sums, degree_arrived, sems[4])
+    degree_copies = sum_start(degree_sums, degree_arrived, sems[6])
     current = mm(factor_inverse(total_finish(0, start_copies)), start[...])
     degree = 1.0 + sum_finish(degree_sums, degree_arrived, degree_copies)[:1]
     scale = 1.0 / jnp.sqrt(degree)
 
-    def operate(stage, value):
-        panel_ref, sum_ref, arrived_ref = panels.at[stage], sums.at[stage], arrived.at[stage]
-        gather_sem, sum_sem = sems[5 + 2 * stage], sems[6 + 2 * stage]
+    half = width_k // HALVES
+
+    def operate(stage, value, early=None, late=None):
         panel = (value * scale).astype(jnp.bfloat16)
-        for v in range(class_tiles):
-            panel_ref[my_col, v] = panel[:, v * TILE : (v + 1) * TILE]
-        copies = [
-            send(
-                panel_ref.at[my_col],
-                panel_ref.at[my_col],
-                gather_sem.at[0, step],
-                gather_sem.at[1, step],
-                {"col": lax.rem(my_col + step, columns)},
-            )
-            for step in range(1, columns)
-        ]
-        sum_ref[...] = jnp.zeros_like(sum_ref)
-        for step in range(columns):
-            if step:
-                copies[step - 1].wait_recv()
-            group = lax.rem(my_col + columns - step, columns)
-
-            def block_step(block, carry):
-                for q in range(Q):
-                    slot = (block * columns + group) * Q + q
-                    base = slot * (class_tiles + 1)
-                    chosen = panel_ref[group, 0]
-                    for u in range(1, class_tiles):
-                        chosen = jnp.where(spots[base] == u, panel_ref[group, u], chosen)
-                    part = jnp.dot(chosen, tiles[slot], preferred_element_type=f32)
-                    for v in range(class_tiles):
-                        sum_ref[block, v] += part * spots[base + 1 + v].astype(f32)
-                return carry
-
-            lax.fori_loop(0, rows, block_step, 0)
-        for copy in copies:
-            copy.wait_send()
-        summed = sum_finish(sum_ref, arrived_ref, sum_start(sum_ref, arrived_ref, sum_sem))
-        return value - scale * (summed + scale * value)
+        gathers = []
+        for h in range(HALVES):
+            panel_ref, sem = panels.at[stage, h], sems[7 + 2 * (HALVES * stage + h)]
+            for v in range(class_tiles):
+                panel_ref[my_col, v] = panel[
+                    h * half : (h + 1) * half, v * TILE : (v + 1) * TILE
+                ]
+            gathers.append(
+                [
+                    send(
+                        panel_ref.at[my_col],
+                        panel_ref.at[my_col],
+                        sem.at[0, step],
+                        sem.at[1, step],
+                        {"col": lax.rem(my_col + step, columns)},
+                    )
+                    for step in range(1, columns)
+                ]
+            )
+        begun = early() if early else None
+        sent_sums = []
+        for h in range(HALVES):
+            panel_ref, sum_ref = panels.at[stage, h], sums.at[stage, h]
+            sum_ref[...] = jnp.zeros_like(sum_ref)
+            for step in range(columns):
+                if step:
+                    gathers[h][step - 1].wait_recv()
+                group = lax.rem(my_col + columns - step, columns)
+
+                def block_step(block, carry):
+                    for q in range(Q):
+                        slot = (block * columns + group) * Q + q
+                        place = lax.rem(tile_rows[slot], class_tiles)
+                        chosen = panel_ref[group, 0]
+                        for u in range(1, class_tiles):
+                            chosen = jnp.where(place == u, panel_ref[group, u], chosen)
+                        part = jnp.dot(chosen, tiles[slot], preferred_element_type=f32)
+                        for v, weight in enumerate(weights(slot, block, q)):
+                            sum_ref[block, v] += part * weight
+                    return carry
+
+                lax.fori_loop(0, rows, block_step, 0)
+            sum_sem = sems[8 + 2 * (HALVES * stage + h)]
+            sent_sums.append(sum_start(sum_ref, arrived.at[stage, h], sum_sem))
+        ended = late(begun) if late else None
+        for copies in gathers:
+            for copy in copies:
+                copy.wait_send()
+        summed = jnp.concatenate(
+            [
+                sum_finish(sums.at[stage, h], arrived.at[stage, h], sent_sums[h])
+                for h in range(HALVES)
+            ],
+            axis=0,
+        )
+        return value - scale * (summed + scale * value), ended
 
     k = width_k
-    imaged = operate(0, current)
+    imaged, _ = operate(0, current)
     rayleigh = sym(total(1, mt(current, imaged) * inverse_total))
     residual = imaged - mm(rayleigh, current)
-    residual_image = operate(1, residual)
-    local = jnp.concatenate(
-        [
-            mt(residual, jnp.concatenate([current, residual], axis=0)),
-            mt(residual, jnp.concatenate([imaged, residual_image], axis=0)),
-            mt(current, jnp.concatenate([residual_image, residual_image], axis=0)),
-        ],
-        axis=1,
-    )
-    sent = total(2, local * inverse_total)
-    g21, g22 = sent[:, :k], sent[:, k : 2 * k]
-    h21 = 0.5 * (sent[:, 2 * k : 3 * k] + sent[:, 4 * k : 5 * k].T)
-    h22 = sym(sent[:, 3 * k : 4 * k])
+
+    def begin_first():
+        rows_here = jnp.concatenate([current, residual, imaged], axis=0)
+        return total_start(2, mt(residual, rows_here) * inverse_total)
+
+    def end_first(copies):
+        known = total_finish(2, copies)
+        g21 = known[:, :k]
+        return known, factor_inverse(known[:, k : 2 * k] - mt(g21, g21))
+
+    residual_image, (known, w22) = operate(1, residual, begin_first, end_first)
+    sent = total(
+        3, mt(residual_image, jnp.concatenate([residual, current], axis=0)) * inverse_total
+    )
+    g21, g22 = known[:, :k], known[:, k : 2 * k]
+    h21 = 0.5 * (known[:, 2 * k :] + sent[:, k:])
+    h22 = sym(sent[:, :k])
     gram = jnp.concatenate(
         [
             jnp.concatenate([eye(k), g21.T], axis=1),
@@ -302,7 +364,6 @@
         ],
         axis=0,
     )
-    w22 = factor_inverse(g22 - mt(g21, g21))
     w21 = -mm(w22, g21)
     inverse = jnp.concatenate(
         [eye(k, 2 * k), jnp.concatenate([w21, w22], axis=1)], axis=0
@@ -321,25 +382,28 @@
     g33 = sym(mt(mm(tail, g22), tail))
 
     residual = imaged - mm(rayleigh, current)
-    residual_image = operate(2, residual)
-    local = jnp.concatenate(
-        [
-            mt(residual, jnp.concatenate([current, residual], axis=0)),
-            mt(residual, jnp.concatenate([imaged, residual_image], axis=0)),
-            mt(residual, jnp.concatenate([previous, previous_image], axis=0)),
-            mt(residual_image, jnp.concatenate([current, previous], axis=0)),
-        ],
-        axis=1,
-    )
-    sent = total(3, local * inverse_total)
-    g21, g22 = sent[:, :k], sent[:, k : 2 * k]
-    h21 = 0.5 * (sent[:, 2 * k : 3 * k] + sent[:, 6 * k : 7 * k])
-    h22 = sym(sent[:, 3 * k : 4 * k])
-    g32 = sent[:, 4 * k : 5 * k].T
-    h32 = 0.5 * (sent[:, 5 * k : 6 * k] + sent[:, 7 * k : 8 * k]).T
-    w22 = factor_inverse(g22 - mt(g21, g21))
-    l32 = mt(g32 - mt(g31, g21), w22)
-    w33 = factor_inverse(g33 - mt(g31, g31) - mt(l32, l32))
+
+    def begin_second():
+        rows_here = jnp.concatenate([current, residual, imaged, previous, previous_image], axis=0)
+        return total_start(4, mt(residual, rows_here) * inverse_total)
+
+    def end_second(copies):
+        known = total_finish(4, copies)
+        g21, g32 = known[:, :k], known[:, 3 * k : 4 * k].T
+        w22 = factor_inverse(known[:, k : 2 * k] - mt(g21, g21))
+        l32 = mt(g32 - mt(g31, g21), w22)
+        return known, w22, l32, factor_inverse(g33 - mt(g31, g31) - mt(l32, l32))
+
+    residual_image, (known, w22, l32, w33) = operate(2, residual, begin_second, end_second)
+    sent = total(
+        5,
+        mt(residual_image, jnp.concatenate([residual, current, previous], axis=0))
+        * inverse_total,
+    )
+    g21 = known[:, :k]
+    h21 = 0.5 * (known[:, 2 * k : 3 * k] + sent[:, k : 2 * k])
+    h22 = sym(sent[:, :k])
+    h32 = 0.5 * (known[:, 4 * k :] + sent[:, 2 * k :]).T
     w21 = -mm(w22, g21)
     w31 = -mm(w33, g31 + mm(l32, w21))
     w32 = -mm(w33, mm(l32, w22))
@@ -371,23 +435,18 @@
     width_k, own = start_block.shape
     class_tiles = own // TILE
     devices = rows * columns
-    slots = tile_values.shape[0]
-    live = jnp.arange(Q, dtype=jnp.int32)[None, :] < pair_counts[0][:, None]
-    live = jnp.broadcast_to(live[:, None, :], (rows, columns, Q)).reshape(slots)
-    here = (tile_column % class_tiles)[:, None] == jnp.arange(class_tiles, dtype=jnp.int32)
-    spots = jnp.concatenate(
-        [(tile_row % class_tiles)[:, None], (here & live[:, None]).astype(jnp.int32)], axis=1
-    ).reshape(-1)
     sizes = (rows, columns, width_k, class_tiles, own * devices)
     flat = devices <= 16
+    half = width_k // HALVES
     scratch = [
-        pltpu.VMEM((3, columns, class_tiles, width_k, TILE), jnp.bfloat16),
-        pltpu.VMEM((3, rows, class_tiles, width_k, TILE), f32),
-        pltpu.VMEM((3, rows, class_tiles, width_k, TILE), f32),
+        pltpu.VMEM((3, HALVES, columns, class_tiles, half, TILE), jnp.bfloat16),
+        pltpu.VMEM((3, HALVES, rows, class_tiles, half, TILE), f32),
+        pltpu.VMEM((3, HALVES, rows, class_tiles, half, TILE), f32),
         pltpu.VMEM((rows, class_tiles, 8, TILE), f32),
         pltpu.VMEM((rows, class_tiles, 8, TILE), f32),
     ]
-    for width in (width_k, width_k, 6 * width_k, 8 * width_k):
+    for blocks in (1, 1, 3, 2, 5, 3):
+        width = blocks * width_k
         if flat:
             scratch += [pltpu.VMEM((devices, width_k // devices, width), f32)] * 3
         else:
@@ -397,24 +456,25 @@
                 pltpu.VMEM((rows, width_k, width), f32),
             ]
     most = devices if flat else max(rows, columns)
-    scratch += [pltpu.SemaphoreType.DMA((4, most))] * 4
+    scratch += [pltpu.SemaphoreType.DMA((4, most))] * 6
     scratch += [pltpu.SemaphoreType.DMA((2, rows))]
-    for stage in range(3):
+    for part in range(3 * HALVES):
         scratch += [pltpu.SemaphoreType.DMA((2, columns)), pltpu.SemaphoreType.DMA((2, rows))]
     vmem = pl.BlockSpec(memory_space=pltpu.VMEM)
+    smem = pl.BlockSpec(memory_space=pltpu.SMEM)
     return pl.pallas_call(
         functools.partial(kernel, sizes),
         out_shape=(
             jax.ShapeDtypeStruct((width_k, own), f32),
             jax.ShapeDtypeStruct((width_k, own), f32),
         ),
-        in_specs=[vmem, pl.BlockSpec(memory_space=pltpu.SMEM), vmem],
+        in_specs=[vmem, smem, smem, smem, vmem],
         out_specs=(vmem, vmem),
         scratch_shapes=scratch,
         compiler_params=pltpu.CompilerParams(
             collective_id=0, has_side_effects=True, vmem_limit_bytes=52 * 1024 * 1024
         ),
-    )(tile_values, spots, start_block)
+    )(tile_values, tile_row, tile_column, pair_counts, start_block)
 
 
 def solution(mesh):

time: 147 us -> 119 us (0.81)
  Pallas kernels: 141 us -> 113 us
  other arithmetic: 2.07 us -> 0 us
  local copies, waits for them, and re-layouts: 3.94 us -> 5.58 us
    pallas_call x1, Pallas kernels: 141 us -> 113 us  [on_device(): pl.pallas_call(functools.partial(kernel, sizes), out_shape=(jax.ShapeDtyp...]
    unnamed x6 -> x12, local copies, waits for them, and re-layouts: 3.62 us -> 5.58 us
where the time goes in v2:
time: 119 us
  Pallas kernels  113 us (95%)
  local copies, waits for them, and re-layouts  5.58 us (5%)
    pallas_call x1, Pallas kernels, on_device(): pl.pallas_call(functools.partial(kernel, sizes), out_shape=(jax.ShapeDtyp...  113 us
    unnamed x12, local copies, waits for them, and re-layouts  5.58 us

profile of v2, /device:TPU:0, one launch (start us, length us, event | category | flops | bytes accessed | tf_op | source)
XLA Modules:
  0.0 119.1 jit_solution(3635691873204822353)
XLA Ops:
  0.6 0.0 copy-start
  0.6 1.4 %copy-done = bf16[48,128,128]{2,1,0:T(8,128)(2,1)S(1)} copy-done((bf16[48,128,128]{2,1,0:T(8,128)(2,1)S(1)}, bf16[48,128,128]{2,1,0:T(8,128)(2,1)}, u32[]{:S(2)}) %copy-start) | copy-done | bytes 1572888
  2.0 0.0 copy-start.1
  2.0 0.9 copy-done.1
  2.9 0.0 copy-start.2
  2.9 0.7 copy-done.2
  3.6 0.0 copy-start.3
  3.6 0.7 copy-done.3
  4.3 0.0 copy-start.4
  4.3 0.7 copy-done.4
  4.9 112.8 %shard_map.68 = (f32[64,512]{1,0:T(8,128)S(1)}, f32[64,512]{1,0:T(8,128)S(1)}) custom-call(bf16[48,128,128]{2,1,0:T(8,128)(2,1)S(1)} %copy-done, s32[48]{0:T(128)S(1)} %copy-done.2, s32[48]{0:T(128)S(1)} %copy-done.3, s32[1,4]{1,0:T(1,128)S(1)} %copy-done.4, f32[64,512]{1,0:T(8,128)S(1)} %copy-done.1), custom_call_target="tpu_custom_call" | custom-call | tf_op jit(solution)/shard_map/pallas_call | solution.py:465
  117.8 0.7 copy.9
  118.4 0.7 copy.10
Async XLA Ops:
  0.6 1.4 %copy-start = (bf16[48,128,128]{2,1,0:T(8,128)(2,1)S(1)}, bf16[48,128,128]{2,1,0:T(8,128)(2,1)}, u32[]{:S(2)}) copy-start(bf16[48,128,128]{2,1,0:T(8,128)(2,1)} %tiles.1) | copy-start | bytes 4718596
  2.0 0.9 copy-start.1
  2.9 0.7 copy-start.2
  3.6 0.7 copy-start.3
  4.3 0.7 copy-start.4
